TPU v7x, 32 devices: a whole 2x2x4 slice. The times are simulated.
32 devices in a mesh: groups: 2 (over x), team: 2 (over core), blk: 8 (over z, y).
Axes of the slice: x: 2, y: 2, z: 4, core: 2. Of those that a mesh axis runs over, the one named last changes fastest.
Arguments:
- probe: bfloat16 [192, 32, 128], P(('groups', 'blk')), parts along dimension 0, may hold values from -6 to 6
- positions: float32 [192, 3, 128], P(('groups', 'blk')), parts along dimension 0, as said below
- conductivity: float32 [192, 128], P(('groups', 'blk')), parts along dimension 0, may hold values from 0.5 to 2
- fluid_exchange: float32 [192, 128], P(('groups', 'blk')), parts along dimension 0, may hold values from 0.5 to 8
- row_blocks: int32 [192], P(('groups', 'blk')), parts along dimension 0, may hold values from 1 to 27, 864 in all
- column_blocks: int32 [192, 27], P(('groups', 'blk')), parts along dimension 0, may hold values from 0 to 95, as said below
Outputs:
- filtered: float32 [192, 32, 128], P(('groups', 'blk')), parts along dimension 0
There are 2 independent parts, one for each index of `groups`. A program takes and returns all parts, laid end to end along the dimension named above; each array names one. Nothing has to cross between parts.
Inputs may be any that keep to these rules, and one draw needn't show every extreme that they name: `row_blocks`: every row lists at least one block; the counts of one bed sum to 864. `column_blocks`: ids in slots at or beyond a row's count are ignored; ids may repeat within a row. Every id differs from its row I by at most 24 around the closed order of the 96 clusters (J = (I + d) mod 96, |d| <= 24), and both ends of that reach occur. `positions`: clusters close in index lie close in space.
All inputs are finite; a program needn't handle non-finite values.
Results may differ from a plain program's by a relative error of at most 0.0029.
Values may be sent and summed in bfloat16 or wider, within the bound.
A program may use at most 64 MiB of HBM per device.

v0:
```python
import functools
import math

import jax
import jax.numpy as jnp
from jax import lax
from jax.experimental import pallas as pl
from jax.experimental.pallas import tpu as pltpu
from jax.sharding import PartitionSpec as P

DEGREE = 8
WIDTH_SQ = 0.245
CENTER = 1.05
HALF_SPAN = 0.95
SCALE = math.sqrt(math.log2(math.e) / WIDTH_SQ)
MESH = pl.DeviceIdType.MESH
REACHES = (-2, -1, 1, 2)


def kernel(
    teams, probe, pos, cond, fluid, counts, cols, out,
    geo, bcast, tiles, even, odd, cur, prev, inv, corr, ids, other,
    geo_send, geo_recv, win_send, win_recv, pair_send, pair_recv,
):
    rows, columns, particles = probe.shape
    half = columns // 2
    slots = cols.shape[1]
    clusters = teams * rows
    group = lax.axis_index("groups")
    member = lax.axis_index("team")
    team = lax.axis_index("blk")

    def at(reach):
        return (group, member, lax.rem(team + reach + teams, teams))

    partner = (group, 1 - member, team)
    barrier = pltpu.get_barrier_semaphore()
    for reach in REACHES:
        pl.semaphore_signal(barrier, inc=1, device_id=at(reach), device_id_type=MESH)
    pl.semaphore_signal(barrier, inc=1, device_id=partner, device_id_type=MESH)

    for r in range(rows):
        geo[2, r, 0:3, :] = pos[r] * SCALE
        geo[2, r, 3:4, :] = 0.5 / cond[r : r + 1, :]
        geo[2, r, 4:8, :] = jnp.zeros((4, particles), jnp.float32)
        mine = probe[r, pl.ds(pl.multiple_of(member * half, half), half), :]
        even[2 * rows + r] = mine
        cur[r] = mine.astype(jnp.float32)
        prev[r] = jnp.zeros((half, particles), jnp.float32)
    pl.semaphore_wait(barrier, len(REACHES) + 1)

    def geo_copy(n):
        reach = REACHES[n]
        return pltpu.make_async_remote_copy(
            src_ref=geo.at[2], dst_ref=geo.at[2 - reach],
            send_sem=geo_send.at[n], recv_sem=geo_recv.at[n],
            device_id=at(reach), device_id_type=MESH,
        )

    def win_copy(parity, n):
        reach = REACHES[n]
        window = (even, odd)[parity]
        return pltpu.make_async_remote_copy(
            src_ref=window.at[pl.ds(2 * rows, rows)], dst_ref=window.at[pl.ds((2 - reach) * rows, rows)],
            send_sem=win_send.at[parity, n], recv_sem=win_recv.at[parity, n],
            device_id=at(reach), device_id_type=MESH,
        )

    for n in range(4):
        geo_copy(n).start()
    for n in range(4):
        win_copy(0, n).start()

    def spread(place):
        def one(r, carry):
            turned = geo[place, r].T
            for k in range(4):
                bcast[place * rows + r, k] = jnp.broadcast_to(
                    turned[:, k : k + 1], (particles, particles)
                )
            return carry
        lax.fori_loop(0, rows, one, 0)

    spread(2)
    for n in range(4):
        geo_copy(n).wait()
        spread(2 - REACHES[n])

    base = (team - 2) * rows

    def build_row(r, carry):
        own = team * rows + r
        count = counts[r]
        xi = [jnp.broadcast_to(geo[2, r, k : k + 1, :], (8, particles)) for k in range(4)]

        def build_tile(s, state):
            total, selves = state
            col = cols[r, s]
            active = s < count
            place = col - base
            place = jnp.where(place < 0, place + clusters, place)
            place = jnp.where(place >= clusters, place - clusters, place)
            place = jnp.where(active, jnp.minimum(place, 5 * rows - 1), 0)
            ids[r, s] = place
            selves = selves + jnp.where(active & (col == own), 1.0, 0.0)
            bias = jnp.where(active, 0.0, -1e30)
            for j in range(0, particles, 16):
                parts = []
                for h in (j, j + 8):
                    dx = bcast[place, 0, h : h + 8, :] - xi[0]
                    dy = bcast[place, 1, h : h + 8, :] - xi[1]
                    dz = bcast[place, 2, h : h + 8, :] - xi[2]
                    power = bias - dx * dx - dy * dy - dz * dz
                    value = jnp.exp2(power) / (bcast[place, 3, h : h + 8, :] + xi[3])
                    total = total + value
                    parts.append(value)
                tiles[r, pl.ds(pl.multiple_of(s * particles + j, 16), 16), :] = jnp.concatenate(
                    parts, 0
                ).astype(jnp.bfloat16)
            return total, selves

        total, selves = lax.fori_loop(
            0, slots, build_tile, (jnp.zeros((8, particles), jnp.float32), jnp.float32(0.0))
        )
        itself = 1.0 / (xi[3] + xi[3])
        degree = jnp.sum(total, axis=0, keepdims=True) - selves * itself[0:1]
        divisor = fluid[pl.ds(r, 1), :] + degree
        inv[r] = jnp.broadcast_to((2.0 / HALF_SPAN) / divisor, (half, particles))
        rounded = itself[0:1].astype(jnp.bfloat16).astype(jnp.float32)
        corr[r] = jnp.broadcast_to(selves * rounded, (half, particles))
        return carry

    lax.fori_loop(0, rows, build_row, 0)

    def step(k, now):
        later = 1 - now
        window, target = (even, odd)[now], (even, odd)[later]
        for n in range(4):
            win_copy(now, n).wait()
        gain = jnp.where(k == 0, 0.5, 1.0)

        def row(r, inner):
            taken = jnp.concatenate(
                [window[ids[r, s]] for s in range(slots)],
                axis=1,
            )
            product = jnp.dot(taken, tiles[r], preferred_element_type=jnp.float32)
            mine = window[2 * rows + r].astype(jnp.float32)
            product = product - corr[r] * mine
            field = cur[r]
            change = (2.0 * (1.0 - CENTER) / HALF_SPAN) * field - product * inv[r]
            fresh = gain * change - prev[r]
            prev[r] = field
            cur[r] = fresh
            target[2 * rows + r] = fresh.astype(jnp.bfloat16)
            return inner

        lax.fori_loop(0, rows, row, 0, unroll=2)

        @pl.when(k < DEGREE - 1)
        def _():
            for n in range(4):
                win_copy(later, n).start()

    def two_steps(i, carry):
        step(2 * i, 0)
        step(2 * i + 1, 1)
        return carry

    lax.fori_loop(0, DEGREE // 2, two_steps, 0)

    swap = pltpu.make_async_remote_copy(
        src_ref=cur, dst_ref=other, send_sem=pair_send, recv_sem=pair_recv,
        device_id=partner, device_id_type=MESH,
    )
    swap.start()
    out[:, pl.ds(pl.multiple_of(member * half, half), half), :] = cur[...]
    swap.wait()
    out[:, pl.ds(pl.multiple_of((1 - member) * half, half), half), :] = other[...]


def local(teams, probe, positions, conductivity, fluid_exchange, row_blocks, column_blocks):
    rows, columns, particles = probe.shape
    slots = column_blocks.shape[1]
    half = columns // 2
    vmem = pl.BlockSpec(memory_space=pltpu.VMEM)
    smem = pl.BlockSpec(memory_space=pltpu.SMEM)
    f32 = jnp.float32
    return pl.pallas_call(
        functools.partial(kernel, teams),
        out_shape=jax.ShapeDtypeStruct((rows, columns, particles), f32),
        in_specs=[vmem, vmem, vmem, vmem, smem, smem],
        out_specs=vmem,
        scratch_shapes=[
            pltpu.VMEM((5, rows, 8, particles), f32),
            pltpu.VMEM((5 * rows, 4, particles, particles), f32),
            pltpu.VMEM((rows, slots * particles, particles), jnp.bfloat16),
            pltpu.VMEM((5 * rows, half, particles), jnp.bfloat16),
            pltpu.VMEM((5 * rows, half, particles), jnp.bfloat16),
            pltpu.VMEM((rows, half, particles), f32),
            pltpu.VMEM((rows, half, particles), f32),
            pltpu.VMEM((rows, half, particles), f32),
            pltpu.VMEM((rows, half, particles), f32),
            pltpu.SMEM((rows, slots), jnp.int32),
            pltpu.VMEM((rows, half, particles), f32),
            pltpu.SemaphoreType.DMA((4,)),
            pltpu.SemaphoreType.DMA((4,)),
            pltpu.SemaphoreType.DMA((2, 4)),
            pltpu.SemaphoreType.DMA((2, 4)),
            pltpu.SemaphoreType.DMA,
            pltpu.SemaphoreType.DMA,
        ],
        compiler_params=pltpu.CompilerParams(
            collective_id=0, has_side_effects=True, vmem_limit_bytes=48 * 1024 * 1024
        ),
    )(probe, positions, conductivity, fluid_exchange, row_blocks, column_blocks)


def solution(mesh):
    return jax.shard_map(
        functools.partial(local, mesh.shape["blk"]),
        mesh=mesh,
        in_specs=(
            P(("groups", "blk"), None, None),
            P(("groups", "blk"), None, None),
            P(("groups", "blk"), None),
            P(("groups", "blk"), None),
            P(("groups", "blk")),
            P(("groups", "blk"), None),
        ),
        out_specs=P(("groups", "blk"), None, None),
        check_vma=False,
    )
```

profile of v0, /device:TPU:0, one launch (start us, length us, event | category | flops | bytes accessed | tf_op | source)
XLA Modules:
  0.0 101.4 jit_solution(9061408680761504530)
XLA Ops:
  0.0 0.0 copy-start
  0.0 0.9 copy-done
  0.9 0.0 copy-start.1
  0.9 0.7 copy-done.1
  1.6 0.0 copy-start.2
  1.6 0.7 copy-done.2
  2.3 0.0 copy-start.3
  2.3 0.7 copy-done.3
  3.0 0.0 copy-start.4
  3.0 0.7 copy-done.4
  3.7 0.0 copy-start.5
  3.7 0.7 copy-done.5
  4.4 96.3 %shard_map.64 = f32[12,32,128]{2,1,0:T(8,128)S(1)} custom-call(bf16[12,32,128]{2,1,0:T(8,128)(2,1)S(1)} %copy-done, f32[12,3,128]{2,1,0:T(4,128)S(1)} %copy-done.1, f32[12,128]{1,0:T(8,128)S(1)} %copy-done.2, f32[12,128]{1,0:T(8,128)S(1)} %copy-done.3, s32[12]{0:T(128)S(1)} %copy-done.5, s32[12,27]{1,0:T(8,128)S(1)} %copy-done.4), custom_call_target="tpu_custom_call" | custom-call | tf_op jit(solution)/shard_map/pallas_call | solution.py:189
  100.7 0.7 copy.8
Async XLA Ops:
  0.0 0.9 copy-start
  0.9 0.7 copy-start.1
  1.6 0.7 copy-start.2
  2.3 0.7 copy-start.3
  3.0 0.7 copy-start.4
  3.7 0.7 copy-start.5
where the time goes:
time: 102 us; the launch traced here: 101 us
  Pallas kernels  96.3 us (94%)
  local copies, waits for them, and re-layouts  5.05 us (5%)
    pallas_call x1, Pallas kernels, local(): pl.pallas_call(functools.partial(kernel, teams), out_shape=jax.ShapeDtype...  96.3 us
    unnamed x13, local copies, waits for them, and re-layouts  5.05 us

commit v1 on v0

--- a/solution.py
+++ b/solution.py
@@ -15,6 +15,7 @@
 SCALE = math.sqrt(math.log2(math.e) / WIDTH_SQ)
 MESH = pl.DeviceIdType.MESH
 REACHES = (-2, -1, 1, 2)
+CHUNK = 4
 
 
 def kernel(
@@ -57,11 +58,12 @@
             device_id=at(reach), device_id_type=MESH,
         )
 
-    def win_copy(parity, n):
+    def win_copy(parity, n, first=0, size=None):
         reach = REACHES[n]
         window = (even, odd)[parity]
+        size = rows if size is None else size
         return pltpu.make_async_remote_copy(
-            src_ref=window.at[pl.ds(2 * rows, rows)], dst_ref=window.at[pl.ds((2 - reach) * rows, rows)],
+            src_ref=window.at[pl.ds(2 * rows + first, size)], dst_ref=window.at[pl.ds((2 - reach) * rows + first, size)],
             send_sem=win_send.at[parity, n], recv_sem=win_recv.at[parity, n],
             device_id=at(reach), device_id_type=MESH,
         )
@@ -73,13 +75,11 @@
 
     def spread(place):
         def one(r, carry):
-            turned = geo[place, r].T
             for k in range(4):
-                bcast[place * rows + r, k] = jnp.broadcast_to(
-                    turned[:, k : k + 1], (particles, particles)
-                )
+                line = geo[place, r, k : k + 1, :]
+                bcast[place * rows + r, k] = jnp.broadcast_to(line, (particles, particles)).T
             return carry
-        lax.fori_loop(0, rows, one, 0)
+        lax.fori_loop(0, rows, one, 0, unroll=2)
 
     spread(2)
     for n in range(4):
@@ -120,7 +120,8 @@
             return total, selves
 
         total, selves = lax.fori_loop(
-            0, slots, build_tile, (jnp.zeros((8, particles), jnp.float32), jnp.float32(0.0))
+            0, slots, build_tile, (jnp.zeros((8, particles), jnp.float32), jnp.float32(0.0)),
+            unroll=3,
         )
         itself = 1.0 / (xi[3] + xi[3])
         degree = jnp.sum(total, axis=0, keepdims=True) - selves * itself[0:1]
@@ -139,7 +140,7 @@
             win_copy(now, n).wait()
         gain = jnp.where(k == 0, 0.5, 1.0)
 
-        def row(r, inner):
+        def row(r):
             taken = jnp.concatenate(
                 [window[ids[r, s]] for s in range(slots)],
                 axis=1,
@@ -153,14 +154,16 @@
             prev[r] = field
             cur[r] = fresh
             target[2 * rows + r] = fresh.astype(jnp.bfloat16)
-            return inner
-
-        lax.fori_loop(0, rows, row, 0, unroll=2)
-
-        @pl.when(k < DEGREE - 1)
-        def _():
-            for n in range(4):
-                win_copy(later, n).start()
+
+        for first in range(0, rows, CHUNK):
+            size = min(CHUNK, rows - first)
+            for r in range(first, first + size):
+                row(r)
+
+            @pl.when(k < DEGREE - 1)
+            def _():
+                for n in range(4):
+                    win_copy(later, n, first, size).start()
 
     def two_steps(i, carry):
         step(2 * i, 0)

time: 102 us -> 82.7 us (0.81)
  Pallas kernels: 96.3 us -> 77.3 us
    pallas_call x1, Pallas kernels: 96.3 us -> 77.3 us  [local(): pl.pallas_call(functools.partial(kernel, teams), out_shape=jax.ShapeDtype...]
where the time goes in v1:
time: 82.7 us; the launch traced here: 82.3 us
  Pallas kernels  77.3 us (93%)
  local copies, waits for them, and re-layouts  5.05 us (6%)
    pallas_call x1, Pallas kernels, local(): pl.pallas_call(functools.partial(kernel, teams), out_shape=jax.ShapeDtype...  77.3 us
    unnamed x13, local copies, waits for them, and re-layouts  5.05 us

profile of v1, /device:TPU:0, one launch (start us, length us, event | category | flops | bytes accessed | tf_op | source)
XLA Modules:
  0.0 82.3 jit_solution(5191185337647977604)
XLA Ops:
  0.0 0.0 copy-start
  0.0 0.9 %copy-done = bf16[12,32,128]{2,1,0:T(8,128)(2,1)S(1)} copy-done((bf16[12,32,128]{2,1,0:T(8,128)(2,1)S(1)}, bf16[12,32,128]{2,1,0:T(8,128)(2,1)}, u32[]{:S(2)}) %copy-start) | copy-done | bytes 98328
  0.9 0.0 copy-start.1
  0.9 0.7 copy-done.1
  1.6 0.0 copy-start.2
  1.6 0.7 copy-done.2
  2.3 0.0 copy-start.3
  2.3 0.7 copy-done.3
  3.0 0.0 copy-start.4
  3.0 0.7 copy-done.4
  3.7 0.0 copy-start.5
  3.7 0.7 copy-done.5
  4.4 77.3 %shard_map.64 = f32[12,32,128]{2,1,0:T(8,128)S(1)} custom-call(bf16[12,32,128]{2,1,0:T(8,128)(2,1)S(1)} %copy-done, f32[12,3,128]{2,1,0:T(4,128)S(1)} %copy-done.1, f32[12,128]{1,0:T(8,128)S(1)} %copy-done.2, f32[12,128]{1,0:T(8,128)S(1)} %copy-done.3, s32[12]{0:T(128)S(1)} %copy-done.5, s32[12,27]{1,0:T(8,128)S(1)} %copy-done.4), custom_call_target="tpu_custom_call" | custom-call | tf_op jit(solution)/shard_map/pallas_call | solution.py:192
  81.6 0.7 copy.8
Async XLA Ops:
  0.0 0.9 %copy-start = (bf16[12,32,128]{2,1,0:T(8,128)(2,1)S(1)}, bf16[12,32,128]{2,1,0:T(8,128)(2,1)}, u32[]{:S(2)}) copy-start(bf16[12,32,128]{2,1,0:T(8,128)(2,1)} %probe.1) | copy-start | bytes 294916
  0.9 0.7 copy-start.1
  1.6 0.7 copy-start.2
  2.3 0.7 copy-start.3
  3.0 0.7 copy-start.4
  3.7 0.7 copy-start.5

commit v2 on v1

--- a/solution.py
+++ b/solution.py
@@ -15,14 +15,26 @@
 SCALE = math.sqrt(math.log2(math.e) / WIDTH_SQ)
 MESH = pl.DeviceIdType.MESH
 REACHES = (-2, -1, 1, 2)
-CHUNK = 4
+CHUNK = 3
 
 
 def kernel(
-    teams, probe, pos, cond, fluid, counts, cols, out,
+    teams, probe_in, pos_in, cond_in, fluid_in, counts_in, cols_in, out,
+    probe, pos, cond, fluid, counts, cols, load_sem,
     geo, bcast, tiles, even, odd, cur, prev, inv, corr, ids, other,
     geo_send, geo_recv, win_send, win_recv, pair_send, pair_recv,
 ):
+    loads = [
+        pltpu.make_async_copy(source, place, load_sem.at[n])
+        for n, (source, place) in enumerate(
+            (
+                (pos_in, pos), (cond_in, cond), (probe_in, probe),
+                (cols_in, cols), (counts_in, counts), (fluid_in, fluid),
+            )
+        )
+    ]
+    for load in loads:
+        load.start()
     rows, columns, particles = probe.shape
     half = columns // 2
     slots = cols.shape[1]
@@ -40,6 +52,8 @@
         pl.semaphore_signal(barrier, inc=1, device_id=at(reach), device_id_type=MESH)
     pl.semaphore_signal(barrier, inc=1, device_id=partner, device_id_type=MESH)
 
+    for load in loads[:3]:
+        load.wait()
     for r in range(rows):
         geo[2, r, 0:3, :] = pos[r] * SCALE
         geo[2, r, 3:4, :] = 0.5 / cond[r : r + 1, :]
@@ -86,6 +100,8 @@
         geo_copy(n).wait()
         spread(2 - REACHES[n])
 
+    for load in loads[3:]:
+        load.wait()
     base = (team - 2) * rows
 
     def build_row(r, carry):
@@ -187,14 +203,21 @@
     slots = column_blocks.shape[1]
     half = columns // 2
     vmem = pl.BlockSpec(memory_space=pltpu.VMEM)
-    smem = pl.BlockSpec(memory_space=pltpu.SMEM)
+    anywhere = pl.BlockSpec(memory_space=pl.ANY)
     f32 = jnp.float32
     return pl.pallas_call(
         functools.partial(kernel, teams),
         out_shape=jax.ShapeDtypeStruct((rows, columns, particles), f32),
-        in_specs=[vmem, vmem, vmem, vmem, smem, smem],
+        in_specs=[anywhere] * 6,
         out_specs=vmem,
         scratch_shapes=[
+            pltpu.VMEM(probe.shape, probe.dtype),
+            pltpu.VMEM(positions.shape, f32),
+            pltpu.VMEM(conductivity.shape, f32),
+            pltpu.VMEM(fluid_exchange.shape, f32),
+            pltpu.SMEM(row_blocks.shape, jnp.int32),
+            pltpu.SMEM(column_blocks.shape, jnp.int32),
+            pltpu.SemaphoreType.DMA((6,)),
             pltpu.VMEM((5, rows, 8, particles), f32),
             pltpu.VMEM((5 * rows, 4, particles, particles), f32),
             pltpu.VMEM((rows, slots * particles, particles), jnp.bfloat16),
@@ -214,7 +237,7 @@
             pltpu.SemaphoreType.DMA,
         ],
         compiler_params=pltpu.CompilerParams(
-            collective_id=0, has_side_effects=True, vmem_limit_bytes=48 * 1024 * 1024
+            collective_id=0, has_side_effects=True, vmem_limit_bytes=60 * 1024 * 1024
         ),
     )(probe, positions, conductivity, fluid_exchange, row_blocks, column_blocks)
 

time: 82.7 us -> 79.4 us (0.960)
  local copies, waits for them, and re-layouts: 5.05 us -> 1.62 us
    unnamed x13 -> x1, local copies, waits for them, and re-layouts: 5.05 us -> 1.62 us
where the time goes in v2:
time: 79.4 us; the launch traced here: 79.2 us
  Pallas kernels  77.6 us (98%)
  local copies, waits for them, and re-layouts  1.62 us (2%)
    pallas_call x1, Pallas kernels, local(): pl.pallas_call(functools.partial(kernel, teams), out_shape=jax.ShapeDtype...  77.6 us
    unnamed x1, local copies, waits for them, and re-layouts  1.62 us

profile of v2, /device:TPU:0, one launch (start us, length us, event | category | flops | bytes accessed | tf_op | source)
XLA Modules:
  0.0 79.2 jit_solution(17921477312286680561)
XLA Ops:
  0.0 77.6 %shard_map.64 = f32[12,32,128]{2,1,0:T(8,128)} custom-call(bf16[12,32,128]{2,1,0:T(8,128)(2,1)} %probe_in.1, f32[12,3,128]{2,1,0:T(4,128)} %pos_in.1, f32[12,128]{1,0:T(8,128)} %cond_in.1, f32[12,128]{1,0:T(8,128)} %fluid_in.1, s32[12]{0:T(128)} %counts_in.1, s32[12,27]{1,0:T(8,128)} %cols_in.1), custom_call_target="tpu_custom_call" | custom-call | tf_op jit(solution)/shard_map/pallas_call | solution.py:208
  77.6 1.6 %copy.8 = f32[12,32,128]{2,1,0:T(8,128)} copy(f32[12,32,128]{2,1,0:T(8,128)} %shard_map.64) | data formatting | bytes 393216

commit v3 on v2

--- a/solution.py
+++ b/solution.py
@@ -57,7 +57,6 @@
     for r in range(rows):
         geo[2, r, 0:3, :] = pos[r] * SCALE
         geo[2, r, 3:4, :] = 0.5 / cond[r : r + 1, :]
-        geo[2, r, 4:8, :] = jnp.zeros((4, particles), jnp.float32)
         mine = probe[r, pl.ds(pl.multiple_of(member * half, half), half), :]
         even[2 * rows + r] = mine
         cur[r] = mine.astype(jnp.float32)
@@ -84,9 +83,6 @@
 
     for n in range(4):
         geo_copy(n).start()
-    for n in range(4):
-        win_copy(0, n).start()
-
     def spread(place):
         def one(r, carry):
             for k in range(4):
@@ -99,6 +95,8 @@
     for n in range(4):
         geo_copy(n).wait()
         spread(2 - REACHES[n])
+    for n in range(4):
+        win_copy(0, n).start()
 
     for load in loads[3:]:
         load.wait()
@@ -218,7 +216,7 @@
             pltpu.SMEM(row_blocks.shape, jnp.int32),
             pltpu.SMEM(column_blocks.shape, jnp.int32),
             pltpu.SemaphoreType.DMA((6,)),
-            pltpu.VMEM((5, rows, 8, particles), f32),
+            pltpu.VMEM((5, rows, 4, particles), f32),
             pltpu.VMEM((5 * rows, 4, particles, particles), f32),
             pltpu.VMEM((rows, slots * particles, particles), jnp.bfloat16),
             pltpu.VMEM((5 * rows, half, particles), jnp.bfloat16),

time: 79.4 us -> 77.9 us (0.981)
  Pallas kernels: 77.6 us -> 76.1 us
    pallas_call x1, Pallas kernels: 77.6 us -> 76.1 us  [local(): pl.pallas_call(functools.partial(kernel, teams), out_shape=jax.ShapeDtype...]
where the time goes in v3:
time: 77.9 us; the launch traced here: 77.7 us
  Pallas kernels  76.1 us (98%)
  local copies, waits for them, and re-layouts  1.62 us (2%)
    pallas_call x1, Pallas kernels, local(): pl.pallas_call(functools.partial(kernel, teams), out_shape=jax.ShapeDtype...  76.1 us
    unnamed x1, local copies, waits for them, and re-layouts  1.62 us

profile of v3, /device:TPU:0, one launch (start us, length us, event | category | flops | bytes accessed | tf_op | source)
XLA Modules:
  0.0 77.7 jit_solution(16956839524899780002)
XLA Ops:
  0.0 76.1 %shard_map.64 = f32[12,32,128]{2,1,0:T(8,128)} custom-call(bf16[12,32,128]{2,1,0:T(8,128)(2,1)} %probe_in.1, f32[12,3,128]{2,1,0:T(4,128)} %pos_in.1, f32[12,128]{1,0:T(8,128)} %cond_in.1, f32[12,128]{1,0:T(8,128)} %fluid_in.1, s32[12]{0:T(128)} %counts_in.1, s32[12,27]{1,0:T(8,128)} %cols_in.1), custom_call_target="tpu_custom_call" | custom-call | tf_op jit(solution)/shard_map/pallas_call | solution.py:206
  76.1 1.6 %copy.8 = f32[12,32,128]{2,1,0:T(8,128)} copy(f32[12,32,128]{2,1,0:T(8,128)} %shard_map.64) | data formatting | bytes 393216
